TPU v7x, 256 devices: a whole 4x4x8 slice. The times are simulated.
256 devices in a mesh: grp: 8 (over x, core), seq: 32 (over z, y).
Axes of the slice: x: 4, y: 4, z: 8, core: 2. Of those that a mesh axis runs over, the one named last changes fastest.
Arguments:
- prompt_keys: bfloat16 [8, 8192, 256], P('grp', 'seq')
- prompt_values: bfloat16 [8, 8192, 256], P('grp', 'seq'), may hold values from -6 to 6
- resp_queries: bfloat16 [8, 4096, 1792], P(None, ('seq', 'grp'))
- resp_keys: bfloat16 [8, 4096, 256], P(None, ('seq', 'grp')), may hold values from -6 to 6
- resp_values: bfloat16 [8, 4096, 256], P(None, ('seq', 'grp')), may hold values from -6 to 6
- segment_ids: int32 [8, 4096], P('grp', 'seq'), may hold values from 0 to 15, never falling along the last dimension, each value on 1 to 512 neighbouring positions
- prompt_lengths: int32 [8], P('grp'), may hold values from 4096 to 8192, as said below
Outputs:
- attended: bfloat16 [8, 4096, 1792], P('grp', 'seq')
Inputs may be any that keep to these rules, and one draw needn't show every extreme that they name: `prompt_lengths`: between half of 8192 and 8192; some group uses all 8192 slots.
All inputs are finite; a program needn't handle non-finite values.
Results may differ from a plain program's by a relative error of at most 0.0095.
Values may be sent and summed in bfloat16 or wider, within the bound.
A program may use at most 64 MiB of HBM per device.

v0:
```python
import math

import jax
import jax.numpy as jnp
from jax import lax
from jax.sharding import PartitionSpec as P

HD = 128
H = 14
KVH = 2
LMAX = 512


masked_score = -1e30


def from_behind(block, axis, distance):
    devices = range(lax.axis_size(axis))
    route = [(i - distance, i) for i in devices if i - distance in devices]
    return lax.ppermute(block, axis, route)


def fold_block(running, queries4, key_block, value_block, valid, scale):
    maxima, totals, weighted = running
    key_count = key_block.shape[0]
    kv_heads = queries4.shape[1]
    keyed = key_block.reshape(key_count, kv_heads, -1)
    valued = value_block.reshape(key_count, kv_heads, -1)
    scores = (
        jnp.einsum("rkgd,nkd->kgrn", queries4, keyed, preferred_element_type=jnp.float32) * scale
    )
    scores = jnp.where(valid, scores, masked_score)
    updated = jnp.maximum(maxima, jnp.max(scores, axis=-1))
    rescale = jnp.exp(maxima - updated)
    weights = jnp.where(valid, jnp.exp(scores - updated[..., None]), 0.0)
    totals = totals * rescale + jnp.sum(weights, axis=-1)
    product = jnp.einsum(
        "kgrn,nkd->kgrd", weights.astype(jnp.bfloat16), valued, preferred_element_type=jnp.float32
    )
    weighted = weighted * rescale[..., None] + product
    return (updated, totals, weighted)


def fold_keys(running, queries4, key_rows, value_rows, first_pos, valid_fn, scale):
    key_count = key_rows.shape[0]
    width = key_rows.shape[1]
    if key_count > 512 and key_count % 512 == 0:
        step_count = key_count // 512

        def step_fn(state, item):
            key_block, value_block, start_pos = item
            positions = start_pos + jnp.arange(512, dtype=jnp.int32)
            return (
                fold_block(state, queries4, key_block, value_block, valid_fn(positions), scale),
                None,
            )

        starts = 512 * jnp.arange(step_count, dtype=jnp.int32)
        items = (
            key_rows.reshape(step_count, 512, width),
            value_rows.reshape(step_count, 512, width),
            starts,
        )
        running, ignored = lax.scan(step_fn, running, items)
        return running
    positions = first_pos + jnp.arange(key_count, dtype=jnp.int32)
    return fold_block(running, queries4, key_rows, value_rows, valid_fn(positions), scale)


def body(
    prompt_keys, prompt_values, resp_queries, resp_keys, resp_values, segment_ids, prompt_lengths
):
    queries, new_keys, new_values = (
        lax.all_to_all(resp_queries, "grp", split_axis=0, concat_axis=1, tiled=True),
        lax.all_to_all(resp_keys, "grp", split_axis=0, concat_axis=1, tiled=True),
        lax.all_to_all(resp_values, "grp", split_axis=0, concat_axis=1, tiled=True),
    )
    queries = queries[0]
    row_count = queries.shape[0]
    heads_group = H // KVH
    scale = 1.0 / math.sqrt(HD)
    queries4 = queries.reshape(row_count, KVH, heads_group, HD)
    first_row = lax.axis_index("seq") * row_count
    row_pos = first_row + jnp.arange(row_count, dtype=jnp.int32)
    whole_segments = lax.all_gather(segment_ids, "seq", axis=1, tiled=True)[0]
    own_segments = segment_ids[0]
    seg_start = jnp.sum((whole_segments[None, :] < own_segments[:, None]).astype(jnp.int32), axis=1)
    prompt_limit = prompt_lengths[0]

    def prompt_valid(positions):
        return jnp.broadcast_to(
            (positions < prompt_limit)[None, :], (row_count, positions.shape[0])
        )

    def reply_valid(positions):
        return (positions[None, :] >= seg_start[:, None]) & (positions[None, :] <= row_pos[:, None])

    initial = (
        jnp.full((KVH, heads_group, row_count), masked_score, jnp.float32),
        jnp.zeros((KVH, heads_group, row_count), jnp.float32),
        jnp.zeros((KVH, heads_group, row_count, HD), jnp.float32),
    )
    running = fold_keys(
        initial,
        queries4,
        lax.all_gather(prompt_keys, "seq", axis=1, tiled=True)[0],
        lax.all_gather(prompt_values, "seq", axis=1, tiled=True)[0],
        jnp.int32(0),
        prompt_valid,
        scale,
    )
    stacked = jnp.stack([new_keys[0], new_values[0]])
    running = fold_keys(running, queries4, stacked[0], stacked[1], first_row, reply_valid, scale)
    reach = min((LMAX + row_count - 2) // row_count, lax.axis_size("seq") - 1)
    for distance in range(1, reach + 1):
        arrived = from_behind(stacked, "seq", distance)
        running = fold_keys(
            running,
            queries4,
            arrived[0],
            arrived[1],
            first_row - distance * row_count,
            reply_valid,
            scale,
        )
    maxima, totals, weighted = running
    output = weighted / totals[..., None]
    return jnp.transpose(output, (2, 0, 1, 3)).reshape(1, row_count, H * HD).astype(jnp.bfloat16)


def solution(mesh):
    in_specs = (
        P("grp", "seq", None),
        P("grp", "seq", None),
        P(None, ("seq", "grp"), None),
        P(None, ("seq", "grp"), None),
        P(None, ("seq", "grp"), None),
        P("grp", "seq"),
        P("grp"),
    )
    out_specs = P("grp", "seq", None)
    return jax.shard_map(body, mesh=mesh, in_specs=in_specs, out_specs=out_specs, check_vma=False)
```

profile of v0, /device:TPU:24, one launch (start us, length us, event | category | flops | bytes accessed | tf_op | source)
XLA Modules:
  0.0 416.3 jit_solution(9731268059820853908)
XLA Ops:
  8.0 4.3 %all-to-all-start.1 = ((bf16[8,16,256]{2,1,0:T(8,128)(2,1)}), bf16[8,16,256]{2,1,0:T(8,128)(2,1)S(1)}, u32[]{:S(2)}, u32[]{:S(2)}) async-start(bf16[8,16,256]{2,1,0:T(8,128)(2,1)} %param.12), calls=%async_computation.1 | async-start | bytes 131072 | tf_op jit(solution)/shard_map/all_to_all | solution.py:75
  12.3 40.0 %all_gather.11 = s32[1,4096]{1,0:T(1,128)S(1)} all-gather(s32[1,128]{1,0:T(1,128)} %param.14), channel_id=1, replica_groups=mesh['grp'=8,'seq'=32] {'seq'}, dimensions={1}, use_global_device_ids=true | all-gather | bytes 16896 | tf_op jit(solution)/shard_map/all_gather | solution.py:85
  53.4 4.8 %all-to-all-start.2 = ((bf16[8,16,256]{2,1,0:T(8,128)(2,1)}), bf16[8,16,256]{2,1,0:T(8,128)(2,1)S(1)}, u32[]{:S(2)}, u32[]{:S(2)}) async-start(bf16[8,16,256]{2,1,0:T(8,128)(2,1)} %param.13), calls=%async_computation.2 | async-start | bytes 131072 | tf_op jit(solution)/shard_map/all_to_all | solution.py:76
  58.2 5.6 %all-to-all-done.2 = bf16[8,16,256]{2,1,0:T(8,128)(2,1)S(1)} async-done(((bf16[8,16,256]{2,1,0:T(8,128)(2,1)}), bf16[8,16,256]{2,1,0:T(8,128)(2,1)S(1)}, u32[]{:S(2)}, u32[]{:S(2)}) %all-to-all-start.2) | async-done | bytes 65568 | tf_op jit(solution)/shard_map/all_to_all | solution.py:76
  63.8 3.5 all-to-all-start
  70.4 4.6 %collective-permute-start.2 = (bf16[2,128,256]{2,1,0:T(8,128)(2,1)S(1)}, bf16[2,128,256]{2,1,0:T(8,128)(2,1)S(1)}, u32[]{:S(2)}, u32[]{:S(2)}) collective-permute-start(bf16[2,128,256]{2,1,0:T(8,128)(2,1)S(1)} %pad_maximum_fusion), channel_id=1, source_target_pairs={{0,3},{1,4},{2,5},{3,6},{4,7},{5,8},{6,9},{7,10},{8,11},{9,12},{10... | collective-permute-start | bytes 393224 | tf_op jit(solution)/shard_map/ppermute | solution.py:20
  75.0 3.2 collective-permute-start.1
  78.2 3.6 collective-permute-start
  82.4 5.5 %collective-permute-done.1 = bf16[2,128,256]{2,1,0:T(8,128)(2,1)S(1)} collective-permute-done((bf16[2,128,256]{2,1,0:T(8,128)(2,1)S(1)}, bf16[2,128,256]{2,1,0:T(8,128)(2,1)S(1)}, u32[]{:S(2)}, u32[]{:S(2)}) %collective-permute-start.1) | collective-permute-done | bytes 131104 | tf_op jit(solution)/shard_map/ppermute | solution.py:20
  88.0 5.1 %collective-permute-done = bf16[2,128,256]{2,1,0:T(8,128)(2,1)S(1)} collective-permute-done((bf16[2,128,256]{2,1,0:T(8,128)(2,1)S(1)}, bf16[2,128,256]{2,1,0:T(8,128)(2,1)S(1)}, u32[]{:S(2)}, u32[]{:S(2)}) %collective-permute-start) | collective-permute-done | bytes 131104 | tf_op jit(solution)/shard_map/ppermute | solution.py:20
  100.1 80.8 %all-gather.5.cloned.1.call-done = bf16[1,8192,256]{2,1,0:T(8,128)(2,1)} async-done(((bf16[1,256,256]{2,1,0:T(8,128)(2,1)}), bf16[1,8192,256]{2,1,0:T(8,128)(2,1)}) %all-gather.5.cloned.1.call-update) | async-done | bytes 4194320 | tf_op jit(solution)/shard_map/all_gather | solution.py:107
  180.9 219.7 %while.15 = (s32[]{:T(128)}, f32[2,7,128]{2,1,0:T(8,128)S(1)}, f32[2,7,128]{2,1,0:T(8,128)S(1)}, f32[2,7,128,128]{3,2,1,0:T(8,128)}, s32[16]{0:T(128)S(1)}, /*in...) while((s32[]{:T(128)}, f32[2,7,128]{2,1,0:T(8,128)S(1)}, ...), condition=%wide.region_3.4_spmd.clone, body=%wide.region_0.3_spmd.clone.sunk | while | flops 482387712 | bytes 16042137 | solution.py:64
  190.0 4.4 %fusion.107 = f32[2,7,128,128]{3,2,1,0:T(8,128)} fusion(bf16[512,2,128,1]{0,2,3,1:T(8,128)(2,1)S(1)} %bitcast.132, f32[2,512,128,7]{2,1,3,0:T(8,128)} %get-tuple-element.239, f32[2,7,128]{2,1,0:T(8,128)S(1)} %select_maximum_fusion.2, pred[512]{0:T(512)(128)(4,1)S(1)} %add_compare_fusion.2, f32[2,7,128,128]{3,2,1,0:T(8,128)} %get-tuple-element.257, ...), kind=kOutput, calls=%fused_computation.10.clone.1 | convolution fusion | flops 240156672 | bytes 5782017 | tf_op jit(solution)/shard_map/while/body/eval_jaxpr/kgrn,nkd->kgrd/dot_general | solution.py:37
  200.3 3.0 fusion.105
  203.5 4.7 %fusion.107 = f32[2,7,128,128]{3,2,1,0:T(8,128)} fusion(bf16[512,2,128,1]{0,2,3,1:T(8,128)(2,1)S(1)} %bitcast.132, f32[2,512,128,7]{2,1,3,0:T(8,128)} %get-tuple-element.239, f32[2,7,128]{2,1,0:T(8,128)S(1)} %select_maximum_fusion.2, pred[512]{0:T(512)(128)(4,1)S(1)} %add_compare_fusion.2, f32[2,7,128,128]{3,2,1,0:T(8,128)} %get-tuple-element.257, ...), kind=kOutput, calls=%fused_computation.10.clone.1 | convolution fusion | flops 240156672 | bytes 5782017 | tf_op jit(solution)/shard_map/while/body/eval_jaxpr/kgrn,nkd->kgrd/dot_general | solution.py:37
  214.0 3.0 fusion.105
  217.2 4.7 %fusion.107 = f32[2,7,128,128]{3,2,1,0:T(8,128)} fusion(bf16[512,2,128,1]{0,2,3,1:T(8,128)(2,1)S(1)} %bitcast.132, f32[2,512,128,7]{2,1,3,0:T(8,128)} %get-tuple-element.239, f32[2,7,128]{2,1,0:T(8,128)S(1)} %select_maximum_fusion.2, pred[512]{0:T(512)(128)(4,1)S(1)} %add_compare_fusion.2, f32[2,7,128,128]{3,2,1,0:T(8,128)} %get-tuple-element.257, ...), kind=kOutput, calls=%fused_computation.10.clone.1 | convolution fusion | flops 240156672 | bytes 5782017 | tf_op jit(solution)/shard_map/while/body/eval_jaxpr/kgrn,nkd->kgrd/dot_general | solution.py:37
  231.0 4.7 %fusion.107 = f32[2,7,128,128]{3,2,1,0:T(8,128)} fusion(bf16[512,2,128,1]{0,2,3,1:T(8,128)(2,1)S(1)} %bitcast.132, f32[2,512,128,7]{2,1,3,0:T(8,128)} %get-tuple-element.239, f32[2,7,128]{2,1,0:T(8,128)S(1)} %select_maximum_fusion.2, pred[512]{0:T(512)(128)(4,1)S(1)} %add_compare_fusion.2, f32[2,7,128,128]{3,2,1,0:T(8,128)} %get-tuple-element.257, ...), kind=kOutput, calls=%fused_computation.10.clone.1 | convolution fusion | flops 240156672 | bytes 5782017 | tf_op jit(solution)/shard_map/while/body/eval_jaxpr/kgrn,nkd->kgrd/dot_general | solution.py:37
  244.7 4.7 %fusion.107 = f32[2,7,128,128]{3,2,1,0:T(8,128)} fusion(bf16[512,2,128,1]{0,2,3,1:T(8,128)(2,1)S(1)} %bitcast.132, f32[2,512,128,7]{2,1,3,0:T(8,128)} %get-tuple-element.239, f32[2,7,128]{2,1,0:T(8,128)S(1)} %select_maximum_fusion.2, pred[512]{0:T(512)(128)(4,1)S(1)} %add_compare_fusion.2, f32[2,7,128,128]{3,2,1,0:T(8,128)} %get-tuple-element.257, ...), kind=kOutput, calls=%fused_computation.10.clone.1 | convolution fusion | flops 240156672 | bytes 5782017 | tf_op jit(solution)/shard_map/while/body/eval_jaxpr/kgrn,nkd->kgrd/dot_general | solution.py:37
  255.3 3.0 fusion.105
  258.5 4.7 %fusion.107 = f32[2,7,128,128]{3,2,1,0:T(8,128)} fusion(bf16[512,2,128,1]{0,2,3,1:T(8,128)(2,1)S(1)} %bitcast.132, f32[2,512,128,7]{2,1,3,0:T(8,128)} %get-tuple-element.239, f32[2,7,128]{2,1,0:T(8,128)S(1)} %select_maximum_fusion.2, pred[512]{0:T(512)(128)(4,1)S(1)} %add_compare_fusion.2, f32[2,7,128,128]{3,2,1,0:T(8,128)} %get-tuple-element.257, ...), kind=kOutput, calls=%fused_computation.10.clone.1 | convolution fusion | flops 240156672 | bytes 5782017 | tf_op jit(solution)/shard_map/while/body/eval_jaxpr/kgrn,nkd->kgrd/dot_general | solution.py:37
  272.2 4.7 %fusion.107 = f32[2,7,128,128]{3,2,1,0:T(8,128)} fusion(bf16[512,2,128,1]{0,2,3,1:T(8,128)(2,1)S(1)} %bitcast.132, f32[2,512,128,7]{2,1,3,0:T(8,128)} %get-tuple-element.239, f32[2,7,128]{2,1,0:T(8,128)S(1)} %select_maximum_fusion.2, pred[512]{0:T(512)(128)(4,1)S(1)} %add_compare_fusion.2, f32[2,7,128,128]{3,2,1,0:T(8,128)} %get-tuple-element.257, ...), kind=kOutput, calls=%fused_computation.10.clone.1 | convolution fusion | flops 240156672 | bytes 5782017 | tf_op jit(solution)/shard_map/while/body/eval_jaxpr/kgrn,nkd->kgrd/dot_general | solution.py:37
  282.8 3.0 fusion.105
  286.0 4.7 %fusion.107 = f32[2,7,128,128]{3,2,1,0:T(8,128)} fusion(bf16[512,2,128,1]{0,2,3,1:T(8,128)(2,1)S(1)} %bitcast.132, f32[2,512,128,7]{2,1,3,0:T(8,128)} %get-tuple-element.239, f32[2,7,128]{2,1,0:T(8,128)S(1)} %select_maximum_fusion.2, pred[512]{0:T(512)(128)(4,1)S(1)} %add_compare_fusion.2, f32[2,7,128,128]{3,2,1,0:T(8,128)} %get-tuple-element.257, ...), kind=kOutput, calls=%fused_computation.10.clone.1 | convolution fusion | flops 240156672 | bytes 5782017 | tf_op jit(solution)/shard_map/while/body/eval_jaxpr/kgrn,nkd->kgrd/dot_general | solution.py:37
  299.7 4.7 %fusion.107 = f32[2,7,128,128]{3,2,1,0:T(8,128)} fusion(bf16[512,2,128,1]{0,2,3,1:T(8,128)(2,1)S(1)} %bitcast.132, f32[2,512,128,7]{2,1,3,0:T(8,128)} %get-tuple-element.239, f32[2,7,128]{2,1,0:T(8,128)S(1)} %select_maximum_fusion.2, pred[512]{0:T(512)(128)(4,1)S(1)} %add_compare_fusion.2, f32[2,7,128,128]{3,2,1,0:T(8,128)} %get-tuple-element.257, ...), kind=kOutput, calls=%fused_computation.10.clone.1 | convolution fusion | flops 240156672 | bytes 5782017 | tf_op jit(solution)/shard_map/while/body/eval_jaxpr/kgrn,nkd->kgrd/dot_general | solution.py:37
  313.5 4.7 %fusion.107 = f32[2,7,128,128]{3,2,1,0:T(8,128)} fusion(bf16[512,2,128,1]{0,2,3,1:T(8,128)(2,1)S(1)} %bitcast.132, f32[2,512,128,7]{2,1,3,0:T(8,128)} %get-tuple-element.239, f32[2,7,128]{2,1,0:T(8,128)S(1)} %select_maximum_fusion.2, pred[512]{0:T(512)(128)(4,1)S(1)} %add_compare_fusion.2, f32[2,7,128,128]{3,2,1,0:T(8,128)} %get-tuple-element.257, ...), kind=kOutput, calls=%fused_computation.10.clone.1 | convolution fusion | flops 240156672 | bytes 5782017 | tf_op jit(solution)/shard_map/while/body/eval_jaxpr/kgrn,nkd->kgrd/dot_general | solution.py:37
  327.2 4.7 %fusion.107 = f32[2,7,128,128]{3,2,1,0:T(8,128)} fusion(bf16[512,2,128,1]{0,2,3,1:T(8,128)(2,1)S(1)} %bitcast.132, f32[2,512,128,7]{2,1,3,0:T(8,128)} %get-tuple-element.239, f32[2,7,128]{2,1,0:T(8,128)S(1)} %select_maximum_fusion.2, pred[512]{0:T(512)(128)(4,1)S(1)} %add_compare_fusion.2, f32[2,7,128,128]{3,2,1,0:T(8,128)} %get-tuple-element.257, ...), kind=kOutput, calls=%fused_computation.10.clone.1 | convolution fusion | flops 240156672 | bytes 5782017 | tf_op jit(solution)/shard_map/while/body/eval_jaxpr/kgrn,nkd->kgrd/dot_general | solution.py:37
  341.0 4.7 %fusion.107 = f32[2,7,128,128]{3,2,1,0:T(8,128)} fusion(bf16[512,2,128,1]{0,2,3,1:T(8,128)(2,1)S(1)} %bitcast.132, f32[2,512,128,7]{2,1,3,0:T(8,128)} %get-tuple-element.239, f32[2,7,128]{2,1,0:T(8,128)S(1)} %select_maximum_fusion.2, pred[512]{0:T(512)(128)(4,1)S(1)} %add_compare_fusion.2, f32[2,7,128,128]{3,2,1,0:T(8,128)} %get-tuple-element.257, ...), kind=kOutput, calls=%fused_computation.10.clone.1 | convolution fusion | flops 240156672 | bytes 5782017 | tf_op jit(solution)/shard_map/while/body/eval_jaxpr/kgrn,nkd->kgrd/dot_general | solution.py:37
  354.7 4.7 %fusion.107 = f32[2,7,128,128]{3,2,1,0:T(8,128)} fusion(bf16[512,2,128,1]{0,2,3,1:T(8,128)(2,1)S(1)} %bitcast.132, f32[2,512,128,7]{2,1,3,0:T(8,128)} %get-tuple-element.239, f32[2,7,128]{2,1,0:T(8,128)S(1)} %select_maximum_fusion.2, pred[512]{0:T(512)(128)(4,1)S(1)} %add_compare_fusion.2, f32[2,7,128,128]{3,2,1,0:T(8,128)} %get-tuple-element.257, ...), kind=kOutput, calls=%fused_computation.10.clone.1 | convolution fusion | flops 240156672 | bytes 5782017 | tf_op jit(solution)/shard_map/while/body/eval_jaxpr/kgrn,nkd->kgrd/dot_general | solution.py:37
  368.5 4.7 %fusion.107 = f32[2,7,128,128]{3,2,1,0:T(8,128)} fusion(bf16[512,2,128,1]{0,2,3,1:T(8,128)(2,1)S(1)} %bitcast.132, f32[2,512,128,7]{2,1,3,0:T(8,128)} %get-tuple-element.239, f32[2,7,128]{2,1,0:T(8,128)S(1)} %select_maximum_fusion.2, pred[512]{0:T(512)(128)(4,1)S(1)} %add_compare_fusion.2, f32[2,7,128,128]{3,2,1,0:T(8,128)} %get-tuple-element.257, ...), kind=kOutput, calls=%fused_computation.10.clone.1 | convolution fusion | flops 240156672 | bytes 5782017 | tf_op jit(solution)/shard_map/while/body/eval_jaxpr/kgrn,nkd->kgrd/dot_general | solution.py:37
  382.2 4.7 %fusion.107 = f32[2,7,128,128]{3,2,1,0:T(8,128)} fusion(bf16[512,2,128,1]{0,2,3,1:T(8,128)(2,1)S(1)} %bitcast.132, f32[2,512,128,7]{2,1,3,0:T(8,128)} %get-tuple-element.239, f32[2,7,128]{2,1,0:T(8,128)S(1)} %select_maximum_fusion.2, pred[512]{0:T(512)(128)(4,1)S(1)} %add_compare_fusion.2, f32[2,7,128,128]{3,2,1,0:T(8,128)} %get-tuple-element.257, ...), kind=kOutput, calls=%fused_computation.10.clone.1 | convolution fusion | flops 240156672 | bytes 5782017 | tf_op jit(solution)/shard_map/while/body/eval_jaxpr/kgrn,nkd->kgrd/dot_general | solution.py:37
  395.9 4.7 %fusion.107 = f32[2,7,128,128]{3,2,1,0:T(8,128)} fusion(bf16[512,2,128,1]{0,2,3,1:T(8,128)(2,1)S(1)} %bitcast.132, f32[2,512,128,7]{2,1,3,0:T(8,128)} %get-tuple-element.239, f32[2,7,128]{2,1,0:T(8,128)S(1)} %select_maximum_fusion.2, pred[512]{0:T(512)(128)(4,1)S(1)} %add_compare_fusion.2, f32[2,7,128,128]{3,2,1,0:T(8,128)} %get-tuple-element.257, ...), kind=kOutput, calls=%fused_computation.10.clone.1 | convolution fusion | flops 240156672 | bytes 5782017 | tf_op jit(solution)/shard_map/while/body/eval_jaxpr/kgrn,nkd->kgrd/dot_general | solution.py:37
  (219 shorter events, 154.2 us)
Async XLA Ops:
  6.5 93.6 %all-gather.3.cloned.1.call-start = ((), (), s32[]{:S(2)}) async-start(), calls=%async_computation.3 | async-start | bytes 4325376 | tf_op jit(solution)/shard_map/all_gather | solution.py:106
  7.3 173.6 %all-gather.5.cloned.1.call-start = ((), (), s32[]{:S(2)}) async-start(), calls=%async_computation.4 | async-start | bytes 4325376 | tf_op jit(solution)/shard_map/all_gather | solution.py:107
  8.0 45.3 %all-to-all-start.1 = ((bf16[8,16,256]{2,1,0:T(8,128)(2,1)}), bf16[8,16,256]{2,1,0:T(8,128)(2,1)S(1)}, u32[]{:S(2)}, u32[]{:S(2)}) async-start(bf16[8,16,256]{2,1,0:T(8,128)(2,1)} %param.12), calls=%async_computation.1 | async-start | bytes 131072 | tf_op jit(solution)/shard_map/all_to_all | solution.py:75
  53.4 10.5 %all-to-all-start.2 = ((bf16[8,16,256]{2,1,0:T(8,128)(2,1)}), bf16[8,16,256]{2,1,0:T(8,128)(2,1)S(1)}, u32[]{:S(2)}, u32[]{:S(2)}) async-start(bf16[8,16,256]{2,1,0:T(8,128)(2,1)} %param.13), calls=%async_computation.2 | async-start | bytes 131072 | tf_op jit(solution)/shard_map/all_to_all | solution.py:76
  63.8 30.0 %all-to-all-start = ((bf16[8,16,1792]{2,1,0:T(8,128)(2,1)}), bf16[8,16,1792]{2,1,0:T(8,128)(2,1)S(1)}, u32[]{:S(2)}, u32[]{:S(2)}) async-start(bf16[8,16,1792]{2,1,0:T(8,128)(2,1)} %param.11), calls=%async_computation | async-start | bytes 917504 | tf_op jit(solution)/shard_map/all_to_all | solution.py:74
  67.3 14.5 %collective-permute-start.3 = (bf16[2,128,256]{2,1,0:T(8,128)(2,1)S(1)}, bf16[2,128,256]{2,1,0:T(8,128)(2,1)S(1)}, u32[]{:S(2)}, u32[]{:S(2)}) collective-permute-start(bf16[2,128,256]{2,1,0:T(8,128)(2,1)S(1)} %pad_maximum_fusion), channel_id=1, source_target_pairs={{0,4},{1,5},{2,6},{3,7},{4,8},{5,9},{6,10},{7,11},{8,12},{9,13},{1... | collective-permute-start | bytes 393224 | tf_op jit(solution)/shard_map/ppermute | solution.py:20
  70.4 11.9 %collective-permute-start.2 = (bf16[2,128,256]{2,1,0:T(8,128)(2,1)S(1)}, bf16[2,128,256]{2,1,0:T(8,128)(2,1)S(1)}, u32[]{:S(2)}, u32[]{:S(2)}) collective-permute-start(bf16[2,128,256]{2,1,0:T(8,128)(2,1)S(1)} %pad_maximum_fusion), channel_id=1, source_target_pairs={{0,3},{1,4},{2,5},{3,6},{4,7},{5,8},{6,9},{7,10},{8,11},{9,12},{10... | collective-permute-start | bytes 393224 | tf_op jit(solution)/shard_map/ppermute | solution.py:20
  75.0 12.9 %collective-permute-start.1 = (bf16[2,128,256]{2,1,0:T(8,128)(2,1)S(1)}, bf16[2,128,256]{2,1,0:T(8,128)(2,1)S(1)}, u32[]{:S(2)}, u32[]{:S(2)}) collective-permute-start(bf16[2,128,256]{2,1,0:T(8,128)(2,1)S(1)} %pad_maximum_fusion), channel_id=1, source_target_pairs={{0,2},{1,3},{2,4},{3,5},{4,6},{5,7},{6,8},{7,9},{8,10},{9,11},{10,... | collective-permute-start | bytes 393224 | tf_op jit(solution)/shard_map/ppermute | solution.py:20
  78.2 15.0 %collective-permute-start = (bf16[2,128,256]{2,1,0:T(8,128)(2,1)S(1)}, bf16[2,128,256]{2,1,0:T(8,128)(2,1)S(1)}, u32[]{:S(2)}, u32[]{:S(2)}) collective-permute-start(bf16[2,128,256]{2,1,0:T(8,128)(2,1)S(1)} %pad_maximum_fusion), channel_id=1, source_target_pairs={{0,1},{1,2},{2,3},{3,4},{4,5},{5,6},{6,7},{7,8},{8,9},{9,10},{10,1... | collective-permute-start | bytes 393224 | tf_op jit(solution)/shard_map/ppermute | solution.py:20
  400.6 4.4 %copy-start = (f32[2,7,128,128]{2,3,1,0:T(8,128)S(1)}, f32[2,7,128,128]{2,3,1,0:T(8,128)}, u32[]{:S(2)}) copy-start(f32[2,7,128,128]{2,3,1,0:T(8,128)} %get-tuple-element.171) | copy-start | bytes 2752516
  403.1 3.5 copy-start.2
  403.1 3.8 copy-start.1
  407.0 1.2 copy-start.3
Sparse Core Ops, SparseCore 0:
  9.9 90.1 all-gather.2
  102.7 78.1 all-gather.4
where the time goes:
time: 420 us; the launch traced here: 416 us
  matrix products  126 us (30%)
  waiting for transfers between devices  99.8 us (24%)
  other arithmetic  72.9 us (17%)
  blocking collectives  40 us (10%)
  local copies, waits for them, and re-layouts  35.9 us (9%)
  starting transfers between devices  26.9 us (6%)
  between operations  13.7 us (3%)
    all_gather x1, waiting for transfers between devices, body(): lax.all_gather(prompt_values, 'seq', axis=1, tiled=True)[0]  80.8 us
    dot_general x21, matrix products, fold_block(): jnp.einsum('kgrn,nkd->kgrd', weights.astype(jnp.bfloat16), valued, prefer...  76 us
    reduce_sum x19, other arithmetic, fold_block(): totals = totals * rescale + jnp.sum(weights, axis=-1)  51.9 us
    dot_general x21, matrix products, fold_block(): jnp.einsum('rkgd,nkd->kgrn', queries4, keyed, preferred_element_type=jnp....  50.3 us
    all_gather x1, blocking collectives, body(): whole_segments = lax.all_gather(segment_ids, 'seq', axis=1, tiled=True)[0]  40 us
    dynamic_slice x64, local copies, waits for them, and re-layouts, fold_keys(): running, ignored = lax.scan(step_fn, running, items)  30.5 us
    lt x16, other arithmetic, prompt_valid(): positions < prompt_limit  19.5 us
    ppermute x4, starting transfers between devices, from_behind(): return lax.ppermute(block, axis, route)  14.2 us
  transfers between devices with their start and end apart: 9, of which 6 were waited for; matrix products, arithmetic and copies ran while one was open for 2% of the time, Pallas kernels for 0%

commit v1 on v0

v1 whole, which is shorter than its diff:
```python
import math

import jax
import jax.numpy as jnp
from jax import lax
from jax.experimental import pallas as pl
from jax.experimental.pallas import tpu as pltpu
from jax.sharding import PartitionSpec as P

HD = 128
H = 14
KVH = 2
HG = H // KVH
WIDE = HG * HD
XS, YS, ZS = 4, 4, 8
ROWS = 256
WIN = 3 * ROWS
SHARD = 256
HALF = 2 * SHARD
CHUNK = 2 * HALF
KEYS = WIN + ZS * CHUNK
MASKED = -1e30
LOG2 = math.log2(math.e) / math.sqrt(HD)
DELTA = (0, -1, 1, -2, 2, -3, 3, 4)
AHEAD = {0: 1, 1: 3, 3: 5, 5: 7}
BEHIND = {0: 2, 2: 4, 4: 6, 6: 7}
STEPS = ((0, 1), (1, 3), (3, 5), (5, 8))
MESH = pl.DeviceIdType.MESH


def kernel(
    pk, pv, rq, rk, rv, seg, plen, out,
    qbuf, kbuf, vbuf, segsrc, segbuf, acc, peak, obuf, bias0,
    q_send, q_recv, rkv_recv, st_send, st_recv,
    ring_send, ring_recv, sib_send, sib_recv,
    fw_send, fw_recv, o_send, o_recv,
):
    gi = lax.axis_index("grp")
    si = lax.axis_index("seq")
    x, c = lax.div(gi, 2), lax.rem(gi, 2)
    z, y = lax.div(si, YS), lax.rem(si, YS)
    yh, yl = lax.div(y, 2), lax.rem(y, 2)
    zn, zp = lax.rem(z + 1, ZS), lax.rem(z + ZS - 1, ZS)
    mine = yh == c
    ahead = (gi, zn * YS + y)
    behind = (gi, zp * YS + y)
    sibling = (2 * x + 1 - c, si)
    next_one = (2 * x + 1 - c, jnp.where(c == 0, si, zn * YS + y))
    prev_one = (2 * x + 1 - c, jnp.where(c == 1, si, zp * YS + y))

    barrier = pltpu.get_barrier_semaphore()

    def greet(i, carry):
        s, g = lax.div(i, 8), lax.rem(i, 8)
        who = z * YS + 2 * c + s

        @pl.when(jnp.logical_or(g != gi, who != si))
        def _():
            pl.semaphore_signal(barrier, inc=1, device_id=(g, who), device_id_type=MESH)

        return carry

    lax.fori_loop(0, 16, greet, 0)
    for who in (ahead, behind, sibling, prev_one):
        pl.semaphore_signal(barrier, inc=1, device_id=who, device_id_type=MESH)
    segsrc[...] = jnp.full((8, 128), plen[0], jnp.int32)
    segsrc[0:1, :] = seg[...]
    pl.semaphore_wait(barrier, jnp.where(mine, 19, 20))

    def remote(src, dst, send, recv, who):
        return pltpu.make_async_remote_copy(
            src_ref=src, dst_ref=dst, send_sem=send, recv_sem=recv,
            device_id=who, device_id_type=MESH,
        )

    def put(src, dst, send, recv, who, here):
        @pl.when(here)
        def _():
            pltpu.make_async_copy(src, dst, recv).start()

        @pl.when(jnp.logical_not(here))
        def _():
            remote(src, dst, send, recv, who).start()

    def sent(src, dst, send, recv, who, here):
        @pl.when(jnp.logical_not(here))
        def _():
            remote(src, dst, send, recv, who).wait_send()

    def arrived(ref, sem):
        pltpu.make_async_copy(ref, ref, sem).wait()

    def keys_at(start, count):
        return kbuf.at[pl.ds(start, count), :]

    def values_at(start, count):
        return vbuf.at[pl.ds(start, count), pl.ds(0, HD)]

    own_at = pl.multiple_of(WIN + y * SHARD, SHARD)

    def staged(h):
        who = (2 * x + yh, z * YS + 2 * c + h)
        here = jnp.logical_and(mine, yl == h)
        cols = pl.ds(h * HD, HD)
        return (
            (pk.at[0, :, cols], keys_at(own_at, SHARD), st_send.at[0, h], st_recv.at[0], who, here),
            (pv.at[0, :, cols], values_at(own_at, SHARD), st_send.at[1, h], st_recv.at[1], who, here),
            (segsrc, segbuf.at[2, yl], st_send.at[2, h], st_recv.at[2], who, here),
        )

    for part in range(3):
        for h in range(2):
            put(*staged(h)[part])

    row_at = pl.multiple_of(yl * 128 + gi * 16, 16)

    def queried(i):
        tx = lax.rem(x + 1 + lax.div(i, 4), XS)
        ty = lax.rem(y + 1 + lax.rem(i, 4), YS)
        th = lax.div(ty, 2)
        tl = lax.rem(ty, 2)
        g = 2 * tx + th
        who = (2 * tx + yh, z * YS + ty)
        here = jnp.logical_and(mine, i == 15)
        wide = pl.ds(pl.multiple_of(tl * WIDE, 128), WIDE)
        cols = pl.ds(pl.multiple_of(tl * HD, 128), HD)
        at = pl.multiple_of(2 * ROWS + row_at, 16)
        return (
            (rq.at[g, :, wide], qbuf.at[pl.ds(row_at, 16), :], q_send.at[0, i], q_recv, who, here),
            (rk.at[g, :, cols], keys_at(at, 16), q_send.at[1, i], rkv_recv.at[0], who, here),
            (rv.at[g, :, cols], values_at(at, 16), q_send.at[2, i], rkv_recv.at[1], who, here),
        )

    def send_queries(i, carry):
        for item in queried(i):
            put(*item)
        return carry

    lax.fori_loop(0, 16, send_queries, 0)

    half_c = pl.multiple_of(c * HALF, HALF)
    other_c = pl.multiple_of((1 - c) * HALF, HALF)

    def chunk_at(kind, r, off):
        start = pl.multiple_of(WIN + r * CHUNK + off, SHARD)
        return keys_at(start, HALF) if kind == 0 else values_at(start, HALF)

    def onward(kind, r):
        moves = []
        if r in AHEAD and not (kind == 1 and AHEAD[r] == 7):
            moves.append((AHEAD[r], ahead))
        if r in BEHIND and not (kind == 0 and BEHIND[r] == 7):
            moves.append((BEHIND[r], behind))
        copies = [
            remote(chunk_at(kind, r, half_c), chunk_at(kind, d, half_c),
                   ring_send.at[kind, d], ring_recv.at[kind, d], who)
            for d, who in moves
        ]
        copies.append(
            remote(chunk_at(kind, r, half_c), chunk_at(kind, r, half_c),
                   sib_send.at[kind, r], sib_recv.at[kind, r], sibling)
        )
        return copies

    def relay(r):
        for kind in range(2):
            sem = st_recv.at[kind] if r == 0 else ring_recv.at[kind, r]
            arrived(chunk_at(kind, r, half_c), sem)
            for copy in onward(kind, r):
                copy.start()

    def from_sibling(r):
        for kind in range(2):
            arrived(chunk_at(kind, r, other_c), sib_recv.at[kind, r])

    relay(0)

    def block_refs(slot):
        return (keys_at(slot * ROWS, ROWS), values_at(slot * ROWS, ROWS), segbuf.at[slot])

    def forwards():
        mine_refs = block_refs(2)
        return [
            remote(mine_refs[k], block_refs(slot)[k], fw_send.at[slot, k], fw_recv.at[slot, k], who)
            for slot, who in ((1, next_one), (0, ahead))
            for k in range(3)
        ]

    arrived(segbuf.at[2], st_recv.at[2])
    arrived(block_refs(2)[0], rkv_recv.at[0])
    arrived(block_refs(2)[1], rkv_recv.at[1])
    for copy in forwards():
        copy.start()

    def ones(i, carry):
        vbuf[pl.ds(pl.multiple_of(i * 256, 256), 256), HD:] = jnp.ones((256, HD), jnp.bfloat16)
        return carry

    lax.fori_loop(0, KEYS // 256, ones, 0)

    limit = segbuf[2, 0, 1:2, :]
    lane = lax.broadcasted_iota(jnp.int32, (1, 128), 1)

    def prompt_bias(r):
        base = lax.rem(z + ZS + DELTA[r], ZS) * CHUNK
        return [
            jnp.where(base + j * 128 + lane < limit, 0.0, MASKED).astype(jnp.float32)
            for j in range(CHUNK // 128)
        ]

    for slot in range(2):
        for k in range(3):
            arrived(block_refs(slot)[k], fw_recv.at[slot, k])

    first = 512 * z + 256 * c - 512
    row = lax.broadcasted_iota(jnp.int32, (128, 128), 0)
    col = lax.broadcasted_iota(jnp.int32, (128, 128), 1)
    for a in range(2):
        ids = jnp.broadcast_to(segbuf[2, a, 0:1, :].astype(jnp.float32), (128, 128))
        ids = jnp.transpose(ids)
        for j in range(WIN // 128):
            theirs = segbuf[j // 2, j % 2, 0:1, :].astype(jnp.float32)
            before = (j * 128 + col <= 512 + a * 128 + row) & (first + j * 128 + col >= 0)
            bias0[a * 128:(a + 1) * 128, j * 128:(j + 1) * 128] = jnp.where(
                before & (ids == theirs), 0.0, MASKED
            ).astype(jnp.float32)

    from_sibling(0)
    arrived(qbuf, q_recv)

    def weigh(lo, count, rows, h, bias):
        q = qbuf[rows, h * HD:(h + 1) * HD]
        s = lax.dot_general(
            q, kbuf[lo:lo + count, :], (((1,), (1,)), ((), ())),
            preferred_element_type=jnp.float32,
        )
        return s + bias

    def numerators(s, top):
        return jnp.exp2((s - top[:, :1]) * LOG2).astype(jnp.bfloat16)

    def product(p, lo, count):
        return jnp.dot(p, vbuf[lo:lo + count, :], preferred_element_type=jnp.float32)

    for step, (a, b) in enumerate(STEPS):
        last = step == len(STEPS) - 1
        pieces = [piece for r in range(a, b) for piece in prompt_bias(r)]
        bias = jnp.concatenate(pieces, axis=1)
        if step == 0:
            lo, count = 0, WIN + CHUNK
            bias = jnp.concatenate(
                [bias0[...], jnp.broadcast_to(bias, (ROWS, CHUNK))], axis=1
            )
        else:
            lo, count = WIN + a * CHUNK, (b - a) * CHUNK
            for r in range(a, b):
                from_sibling(r)
        if not last:
            for h in range(HG):
                if h == 3:
                    relay(b)
                    relay(b + 1)
                if h == 6 and step == 2:
                    relay(7)
                rows = slice(0, ROWS)
                s = weigh(lo, count, rows, h, bias)
                top = jnp.max(s, axis=1, keepdims=True)
                if step == 0:
                    top = jnp.broadcast_to(top, (ROWS, HD))
                    acc[h] = product(numerators(s, top), lo, count)
                else:
                    old = peak[h]
                    top = jnp.maximum(old, top)
                    fade = jnp.exp2((old - top) * LOG2)
                    got = product(numerators(s, top), lo, count)
                    acc[h, :, :HD] = acc[h, :, :HD] * fade + got[:, :HD]
                    acc[h, :, HD:] = acc[h, :, HD:] * fade + got[:, HD:]
                peak[h] = top
        else:
            for a_half in range(2):
                for h in range(HG):
                    rows = slice(a_half * 128, a_half * 128 + 128)
                    s = weigh(lo, count, rows, h, bias)
                    old = peak[h, rows, :]
                    top = jnp.maximum(old, jnp.max(s, axis=1, keepdims=True))
                    fade = jnp.exp2((old - top) * LOG2)
                    got = product(numerators(s, top), lo, count)
                    weighted = acc[h, rows, :HD] * fade + got[:, :HD]
                    total = acc[h, rows, HD:] * fade + got[:, HD:]
                    obuf[a_half, h] = (weighted / total).astype(jnp.bfloat16)
                    put(*answer(obuf, out, o_send, o_recv, a_half, h, x, c, z, yh, yl, mine))

    for a_half in range(2):
        for h in range(HG):
            sent(*answer(obuf, out, o_send, o_recv, a_half, h, x, c, z, yh, yl, mine))
    for h in range(2):
        for item in staged(h):
            sent(*item)

    def settle(i, carry):
        for item in queried(i):
            sent(*item)
        return carry

    lax.fori_loop(0, 16, settle, 0)
    for r in range(ZS):
        for kind in range(2):
            for copy in onward(kind, r):
                copy.wait_send()
    for copy in forwards():
        copy.wait_send()
    arrived(out, o_recv)


def answer(obuf, out, o_send, o_recv, a_half, h, x, c, z, yh, yl, mine):
    who = (2 * x + yh, z * YS + 2 * c + a_half)
    here = jnp.logical_and(mine, yl == a_half)
    cols = pl.ds(pl.multiple_of(yl * WIDE + h * HD, 128), HD)
    return (obuf.at[a_half, h], out.at[0, :, cols], o_send.at[a_half, h], o_recv, who, here)


def body(
    prompt_keys, prompt_values, resp_queries, resp_keys, resp_values, segment_ids, prompt_lengths
):
    dma = pltpu.SemaphoreType.DMA
    held = pl.BlockSpec(memory_space=pl.ANY)
    return pl.pallas_call(
        kernel,
        out_shape=jax.ShapeDtypeStruct((1, 128, H * HD), jnp.bfloat16),
        in_specs=[held] * 5
        + [pl.BlockSpec(memory_space=pltpu.VMEM), pl.BlockSpec(memory_space=pltpu.SMEM)],
        out_specs=held,
        scratch_shapes=[
            pltpu.VMEM((ROWS, WIDE), jnp.bfloat16),
            pltpu.VMEM((KEYS, HD), jnp.bfloat16),
            pltpu.VMEM((KEYS, 2 * HD), jnp.bfloat16),
            pltpu.VMEM((8, 128), jnp.int32),
            pltpu.VMEM((3, 2, 8, 128), jnp.int32),
            pltpu.VMEM((HG, ROWS, 2 * HD), jnp.float32),
            pltpu.VMEM((HG, ROWS, HD), jnp.float32),
            pltpu.VMEM((2, HG, 128, HD), jnp.bfloat16),
            pltpu.VMEM((ROWS, WIN), jnp.float32),
            dma((3, 16)),
            dma,
            dma((2,)),
            dma((3, 2)),
            dma((3,)),
            dma((2, ZS)),
            dma((2, ZS)),
            dma((2, ZS)),
            dma((2, ZS)),
            dma((2, 3)),
            dma((2, 3)),
            dma((2, HG)),
            dma,
        ],
        compiler_params=pltpu.CompilerParams(
            collective_id=0, has_side_effects=True, vmem_limit_bytes=50 << 20
        ),
        name="shared_prompt_attention",
    )(prompt_keys, prompt_values, resp_queries, resp_keys, resp_values, segment_ids, prompt_lengths)


def solution(mesh):
    in_specs = (
        P("grp", "seq", None),
        P("grp", "seq", None),
        P(None, ("seq", "grp"), None),
        P(None, ("seq", "grp"), None),
        P(None, ("seq", "grp"), None),
        P("grp", "seq"),
        P("grp"),
    )
    out_specs = P("grp", "seq", None)
    return jax.shard_map(body, mesh=mesh, in_specs=in_specs, out_specs=out_specs, check_vma=False)
```

time: 420 us -> 80.7 us (0.19)
  matrix products: 126 us -> 0 us
  waiting for transfers between devices: 99.8 us -> 0 us
  Pallas kernels: 0 us -> 74.5 us
  other arithmetic: 72.9 us -> 0 us
  blocking collectives: 40 us -> 0 us
  local copies, waits for them, and re-layouts: 35.9 us -> 5.27 us
  starting transfers between devices: 26.9 us -> 0 us
  between operations: 13.7 us -> 0.7 us
    dot_general x42 -> x0, matrix products: 126 us -> none  [the longest x21 76 us: fold_block(): jnp.einsum('kgrn,nkd->kgrd', weights.astype(jnp.bfloat16), valued, prefer...]
    all_gather x2 -> x0, waiting for transfers between devices: 81.8 us -> none  [the longest x1 80.8 us: body(): lax.all_gather(prompt_values, 'seq', axis=1, tiled=True)[0]]
    pallas_call x0 -> x1, Pallas kernels: none -> 74.5 us  [body(): pl.pallas_call(kernel, out_shape=jax.ShapeDtypeStruct((1, 128, H * HD), j...]
    reduce_sum x20 -> x0, other arithmetic: 52.9 us -> none  [the longest x19 51.9 us: fold_block(): totals = totals * rescale + jnp.sum(weights, axis=-1)]
    all_gather x1 -> x0, blocking collectives: 40 us -> none  [body(): whole_segments = lax.all_gather(segment_ids, 'seq', axis=1, tiled=True)[0]]
    dynamic_slice x64 -> x0, local copies, waits for them, and re-layouts: 30.5 us -> none  [fold_keys(): running, ignored = lax.scan(step_fn, running, items)]
    lt x16 -> x0, other arithmetic: 19.5 us -> none  [prompt_valid(): positions < prompt_limit]
    ppermute x4 -> x0, starting transfers between devices: 14.2 us -> none  [from_behind(): return lax.ppermute(block, axis, route)]
  transfers between devices with their start and end apart: 9 -> 0, of which waited for: 6 -> 0; matrix products, arithmetic and copies ran while one was open for 2% -> 0% of each run, Pallas kernels for 0% -> 0%
where the time goes in v1:
time: 80.7 us; the launch traced here: 80.5 us
  Pallas kernels  74.5 us (92%)
  local copies, waits for them, and re-layouts  5.27 us (7%)
    pallas_call x1, Pallas kernels, body(): pl.pallas_call(kernel, out_shape=jax.ShapeDtypeStruct((1, 128, H * HD), j...  74.5 us
    unnamed x13, local copies, waits for them, and re-layouts  5.27 us

profile of v1, /device:TPU:24, one launch (start us, length us, event | category | flops | bytes accessed | tf_op | source)
XLA Modules:
  0.0 80.5 jit_solution(13345753576090647014)
XLA Ops:
  0.0 0.0 copy-start.5
  0.7 0.0 copy-done.5
  0.7 0.0 copy-start
  0.7 1.0 %copy-done = bf16[8,16,1792]{2,1,0:T(8,128)(2,1)S(1)} copy-done((bf16[8,16,1792]{2,1,0:T(8,128)(2,1)S(1)}, bf16[8,16,1792]{2,1,0:T(8,128)(2,1)}, u32[]{:S(2)}) %copy-start) | copy-done | bytes 458776
  1.7 0.0 copy-start.1
  1.7 0.9 %copy-done.1 = bf16[1,256,256]{2,1,0:T(8,128)(2,1)S(1)} copy-done((bf16[1,256,256]{2,1,0:T(8,128)(2,1)S(1)}, bf16[1,256,256]{2,1,0:T(8,128)(2,1)}, u32[]{:S(2)}) %copy-start.1) | copy-done | bytes 131096
  2.6 0.0 copy-start.2
  2.6 0.9 %copy-done.2 = bf16[1,256,256]{2,1,0:T(8,128)(2,1)S(1)} copy-done((bf16[1,256,256]{2,1,0:T(8,128)(2,1)S(1)}, bf16[1,256,256]{2,1,0:T(8,128)(2,1)}, u32[]{:S(2)}) %copy-start.2) | copy-done | bytes 131096
  3.5 0.0 copy-start.3
  3.5 0.8 %copy-done.3 = bf16[8,16,256]{2,1,0:T(8,128)(2,1)S(1)} copy-done((bf16[8,16,256]{2,1,0:T(8,128)(2,1)S(1)}, bf16[8,16,256]{2,1,0:T(8,128)(2,1)}, u32[]{:S(2)}) %copy-start.3) | copy-done | bytes 65560
  4.3 0.0 copy-start.4
  4.3 0.8 %copy-done.4 = bf16[8,16,256]{2,1,0:T(8,128)(2,1)S(1)} copy-done((bf16[8,16,256]{2,1,0:T(8,128)(2,1)S(1)}, bf16[8,16,256]{2,1,0:T(8,128)(2,1)}, u32[]{:S(2)}) %copy-start.4) | copy-done | bytes 65560
  5.2 74.5 %shared_prompt_attention.1 = bf16[1,128,1792]{2,1,0:T(8,128)(2,1)S(1)} custom-call(bf16[1,256,256]{2,1,0:T(8,128)(2,1)S(1)} %copy-done.1, bf16[1,256,256]{2,1,0:T(8,128)(2,1)S(1)} %copy-done.2, bf16[8,16,1792]{2,1,0:T(8,128)(2,1)S(1)} %copy-done, bf16[8,16,256]{2,1,0:T(8,128)(2,1)S(1)} %copy-done.3, bf16[8,16,256]{2,1,0:T(8,128)(2,1)S(1)} %copy-done.4, ...), custom_call_target="tpu_custom_call" | custom-call | tf_op jit(solution)/shard_map/shared_prompt_attention/pallas_call | solution.py:327
  79.7 0.8 copy.10
Async XLA Ops:
  0.0 0.7 copy-start.5
  0.7 1.0 %copy-start = (bf16[8,16,1792]{2,1,0:T(8,128)(2,1)S(1)}, bf16[8,16,1792]{2,1,0:T(8,128)(2,1)}, u32[]{:S(2)}) copy-start(bf16[8,16,1792]{2,1,0:T(8,128)(2,1)} %rq.1) | copy-start | bytes 1376260
  1.7 0.9 %copy-start.1 = (bf16[1,256,256]{2,1,0:T(8,128)(2,1)S(1)}, bf16[1,256,256]{2,1,0:T(8,128)(2,1)}, u32[]{:S(2)}) copy-start(bf16[1,256,256]{2,1,0:T(8,128)(2,1)} %pk.1) | copy-start | bytes 393220
  2.6 0.9 %copy-start.2 = (bf16[1,256,256]{2,1,0:T(8,128)(2,1)S(1)}, bf16[1,256,256]{2,1,0:T(8,128)(2,1)}, u32[]{:S(2)}) copy-start(bf16[1,256,256]{2,1,0:T(8,128)(2,1)} %pv.1) | copy-start | bytes 393220
  3.5 0.8 %copy-start.3 = (bf16[8,16,256]{2,1,0:T(8,128)(2,1)S(1)}, bf16[8,16,256]{2,1,0:T(8,128)(2,1)}, u32[]{:S(2)}) copy-start(bf16[8,16,256]{2,1,0:T(8,128)(2,1)} %rk.1) | copy-start | bytes 196612
  4.3 0.8 %copy-start.4 = (bf16[8,16,256]{2,1,0:T(8,128)(2,1)S(1)}, bf16[8,16,256]{2,1,0:T(8,128)(2,1)}, u32[]{:S(2)}) copy-start(bf16[8,16,256]{2,1,0:T(8,128)(2,1)} %rv.1) | copy-start | bytes 196612

commit v2 on v1

v2 whole, which is shorter than its diff:
```python
import math

import jax
import jax.numpy as jnp
from jax import lax
from jax.experimental import pallas as pl
from jax.experimental.pallas import tpu as pltpu
from jax.sharding import PartitionSpec as P

HD = 128
H = 14
KVH = 2
HG = H // KVH
WIDE = HG * HD
XS, YS, ZS = 4, 4, 8
ROWS = 256
WIN = 3 * ROWS
SHARD = 256
HALF = 2 * SHARD
CHUNK = 2 * HALF
KEYS = WIN + ZS * CHUNK
MASKED = -1e30
LOG2 = math.log2(math.e) / math.sqrt(HD)
DELTA = (0, -1, 1, -2, 2, -3, 3, 4)
AHEAD = {0: 1, 1: 3, 3: 5}
BEHIND = {0: 2, 2: 4, 4: 6}
TAIL = 7 * CHUNK
OWN = (0, 1024, 1536, 3072, 3584, 5120, 5632, TAIL + 128)
SIB = (512, 2048, 2560, 4096, 4608, 6144, 6656, TAIL + 640)
WINDOW = ((TAIL, 128), (TAIL + 1152, 128), (TAIL + 1280, 256), (TAIL + 1536, 256))
STEPS = ((0, 1), (1, 3), (3, 5), (5, 7))
PARTS = ((0, 0), (0, 1), (1, 0), (1, 1))
KEY_PARTS, VALUE_PARTS = PARTS[:2], PARTS[2:]


def moves_of(parts, *chunks):
    return tuple((kind, part, r) for kind, part in parts for r in chunks)


FIRST = moves_of(PARTS, 0) + moves_of(KEY_PARTS, 1, 2)
RELAYS = {
    (0, 3): moves_of(VALUE_PARTS, 1, 2),
    (1, 5): moves_of(PARTS, 3, 4) + ("send",),
    (2, 5): moves_of(PARTS, 5, 6),
    (3, 4): ("cross",) + moves_of(PARTS, 7),
}
ANSWERS = ((0, 0, 7), (1, 0, 4), (1, 4, 7))
MESH = pl.DeviceIdType.MESH


def kernel(
    pk, pv, rq, rk, rv, seg, plen, out,
    qbuf, kbuf, vbuf, segsrc, segbuf, acc, peak, obuf, bias0,
    q_send, q_recv, rkv_recv, st_send, st_recv,
    ring_send, ring_recv, sib_send, sib_recv,
    fw_send, fw_recv, o_send, o_recv,
):
    gi = lax.axis_index("grp")
    si = lax.axis_index("seq")
    x, c = lax.div(gi, 2), lax.rem(gi, 2)
    z, y = lax.div(si, YS), lax.rem(si, YS)
    yh, yl = lax.div(y, 2), lax.rem(y, 2)
    zn, zp = lax.rem(z + 1, ZS), lax.rem(z + ZS - 1, ZS)
    mine = yh == c
    ahead = (gi, zn * YS + y)
    behind = (gi, zp * YS + y)
    sibling = (2 * x + 1 - c, si)

    barrier = pltpu.get_barrier_semaphore()

    def greet(i, carry):
        s, g = lax.div(i, 8), lax.rem(i, 8)
        who = z * YS + 2 * c + s

        @pl.when(jnp.logical_or(g != gi, who != si))
        def _():
            pl.semaphore_signal(barrier, inc=1, device_id=(g, who), device_id_type=MESH)

        return carry

    lax.fori_loop(0, 16, greet, 0)
    for who in (ahead, behind, sibling):
        pl.semaphore_signal(barrier, inc=1, device_id=who, device_id_type=MESH)
    segsrc[...] = jnp.full((8, 128), plen[0], jnp.int32)
    segsrc[0:1, :] = seg[...]
    pl.semaphore_wait(barrier, jnp.where(mine, 18, 19))

    def remote(src, dst, send, recv, who):
        return pltpu.make_async_remote_copy(
            src_ref=src, dst_ref=dst, send_sem=send, recv_sem=recv,
            device_id=who, device_id_type=MESH,
        )

    def put(src, dst, send, recv, who, here):
        @pl.when(here)
        def _():
            pltpu.make_async_copy(src, dst, recv).start()

        @pl.when(jnp.logical_not(here))
        def _():
            remote(src, dst, send, recv, who).start()

    def sent(src, dst, send, recv, who, here):
        @pl.when(jnp.logical_not(here))
        def _():
            remote(src, dst, send, recv, who).wait_send()

    def arrived(ref, sem):
        pltpu.make_async_copy(ref, ref, sem).wait()

    def keys_at(start, count):
        return kbuf.at[pl.ds(start, count), :]

    def values_at(start, count):
        return vbuf.at[pl.ds(start, count), pl.ds(0, HD)]

    own_at = pl.multiple_of(OWN[0] + yl * SHARD, SHARD)

    def staged(h):
        who = (2 * x + yh, z * YS + 2 * c + h)
        here = jnp.logical_and(mine, yl == h)
        cols = pl.ds(h * HD, HD)
        return (
            (pk.at[0, :, cols], keys_at(own_at, SHARD), st_send.at[0, h], st_recv.at[0, yl], who, here),
            (pv.at[0, :, cols], values_at(own_at, SHARD), st_send.at[1, h], st_recv.at[1, yl], who, here),
            (segsrc, segbuf.at[2, yl], st_send.at[2, h], st_recv.at[2, yl], who, here),
        )

    row_at = pl.multiple_of(yl * 128 + gi * 16, 16)

    def queried(i):
        tx = lax.rem(x + 1 + lax.div(i, 4), XS)
        ty = lax.rem(y + 1 + lax.rem(i, 4), YS)
        th = lax.div(ty, 2)
        tl = lax.rem(ty, 2)
        g = 2 * tx + th
        who = (2 * tx + yh, z * YS + ty)
        here = jnp.logical_and(mine, i == 15)
        wide = pl.ds(pl.multiple_of(tl * WIDE, 128), WIDE)
        cols = pl.ds(pl.multiple_of(tl * HD, 128), HD)
        at = pl.multiple_of(WINDOW[3][0] + row_at, 16)
        return (
            (rq.at[g, :, wide], qbuf.at[pl.ds(row_at, 16), :], q_send.at[0, i], q_recv, who, here),
            (rk.at[g, :, cols], keys_at(at, 16), q_send.at[1, i], rkv_recv.at[0], who, here),
            (rv.at[g, :, cols], values_at(at, 16), q_send.at[2, i], rkv_recv.at[1], who, here),
        )

    def send_queries(i, carry):
        put(*queried(i)[0])
        return carry

    def send_rest(i, carry):
        put(*queried(i)[1])
        put(*queried(i)[2])
        return carry

    for part in range(3):
        for h in range(2):
            put(*staged(h)[part])
    lax.fori_loop(0, 16, send_queries, 0)
    lax.fori_loop(0, 16, send_rest, 0)

    def ones(i, carry):
        vbuf[pl.ds(pl.multiple_of(i * 256, 256), 256), HD:] = jnp.ones((256, HD), jnp.bfloat16)
        return carry

    lax.fori_loop(0, KEYS // 256, ones, 0)

    def rows_of(kind, start, count):
        return keys_at(start, count) if kind == 0 else values_at(start, count)

    def piece_at(kind, start, part):
        return rows_of(kind, start + part * SHARD, SHARD)

    def onward(kind, part, r):
        here = piece_at(kind, OWN[r], part)
        moves = [(way[r], who) for way, who in ((AHEAD, ahead), (BEHIND, behind)) if r in way]
        if (r == 5 and (kind, part) == (0, 0)) or (r == 6 and (kind, part) != (0, 0)):
            moves.append((7, ahead if r == 5 else behind))
        copies = [
            remote(here, piece_at(kind, OWN[to], part), ring_send.at[kind, part, to],
                   ring_recv.at[kind, part, to], who)
            for to, who in moves
        ]
        copies.append(remote(
            here, piece_at(kind, SIB[r], part), sib_send.at[kind, part, r],
            sib_recv.at[kind, part, r], sibling,
        ))
        return copies

    def relay(kind, part, r):
        sem = st_recv.at[kind, part] if r == 0 else ring_recv.at[kind, part, r]
        arrived(piece_at(kind, OWN[r], part), sem)
        for copy in onward(kind, part, r):
            copy.start()

    def from_sibling(r):
        for kind in range(2):
            for part in range(2):
                arrived(piece_at(kind, SIB[r], part), sib_recv.at[kind, part, r])

    for item in FIRST:
        relay(*item)

    def forwards():
        copies = []
        for kind in range(2):
            for part in range(2):
                src = WINDOW[3][0] + 128 * part
                copies.append(remote(
                    rows_of(kind, src, 128), rows_of(kind, WINDOW[part][0], 128),
                    fw_send.at[kind, part], fw_recv.at[kind, part], ahead,
                ))
        copies.append(
            remote(segbuf.at[2], segbuf.at[0], fw_send.at[2, 0], fw_recv.at[2, 0], ahead)
        )
        return copies

    def crossings():
        copies = []
        for kind in range(2):
            for part in range(2):
                src = jnp.where(c == 0, WINDOW[3][0] + 128 * part, WINDOW[part][0])
                src = pl.multiple_of(src, 128)
                copies.append(remote(
                    rows_of(kind, src, 128), rows_of(kind, WINDOW[2][0] + 128 * part, 128),
                    fw_send.at[kind, 2 + part], fw_recv.at[kind, 2 + part], sibling,
                ))
        src = segbuf.at[jnp.where(c == 0, 2, 0)]
        copies.append(remote(src, segbuf.at[1], fw_send.at[2, 1], fw_recv.at[2, 1], sibling))
        return copies

    def send_window():
        for kind in range(2):
            arrived(rows_of(kind, *WINDOW[3]), rkv_recv.at[kind])
        for copy in forwards():
            copy.start()

    def cross_window():
        for kind in range(2):
            for part in range(2):
                arrived(rows_of(kind, *WINDOW[part]), fw_recv.at[kind, part])
        arrived(segbuf.at[0], fw_recv.at[2, 0])
        for copy in crossings():
            copy.start()

    def take_window():
        for kind in range(2):
            for part in range(2):
                start = WINDOW[2][0] + 128 * part
                arrived(rows_of(kind, start, 128), fw_recv.at[kind, 2 + part])
        arrived(segbuf.at[1], fw_recv.at[2, 1])
        first = 512 * z + 256 * c - 512
        row = lax.broadcasted_iota(jnp.int32, (128, 128), 0)
        col = lax.broadcasted_iota(jnp.int32, (128, 128), 1)
        for a in range(2):
            ids = jnp.broadcast_to(segbuf[2, a, 0:1, :].astype(jnp.float32), (128, 128))
            ids = jnp.transpose(ids)
            for j in range(WIN // 128):
                theirs = segbuf[j // 2, j % 2, 0:1, :].astype(jnp.float32)
                before = (j * 128 + col <= 512 + a * 128 + row) & (first + j * 128 + col >= 0)
                bias0[a * 128:(a + 1) * 128, j * 128:(j + 1) * 128] = jnp.where(
                    before & (ids == theirs), 0.0, MASKED
                ).astype(jnp.float32)

    lane = lax.broadcasted_iota(jnp.int32, (1, 128), 1)

    def prompt_bias(r, half):
        limit = segbuf[2, 0, 1:2, :]
        base = lax.rem(z + ZS + DELTA[r], ZS) * CHUNK + half * HALF
        return [
            jnp.where(base + j * 128 + lane < limit, 0.0, MASKED).astype(jnp.float32)
            for j in range(HALF // 128)
        ]

    def weigh(lo, count, rows, h, bias):
        q = qbuf[rows, h * HD:(h + 1) * HD]
        s = lax.dot_general(
            q, kbuf[lo:lo + count, :], (((1,), (1,)), ((), ())),
            preferred_element_type=jnp.float32,
        )
        return s + bias

    def numerators(s, top):
        return jnp.exp2((s - top[:, :1]) * LOG2).astype(jnp.bfloat16)

    def product(p, lo, count):
        return jnp.dot(p, vbuf[lo:lo + count, :], preferred_element_type=jnp.float32)

    def carry_on(item):
        if item == "send":
            send_window()
        elif item == "cross":
            cross_window()
        else:
            relay(*item)

    for j in range(2):
        arrived(segbuf.at[2, j], st_recv.at[2, j])
    arrived(qbuf, q_recv)

    for step, (a, b) in enumerate(STEPS):
        for r in range(a, b):
            from_sibling(r)
        pieces = [
            piece
            for half in (c, 1 - c)
            for r in range(a, b)
            for piece in prompt_bias(r, half)
        ]
        bias = jnp.concatenate(pieces, axis=1)
        lo, count = a * CHUNK, (b - a) * CHUNK
        for h in range(HG):
            rows = slice(0, ROWS)
            s = weigh(lo, count, rows, h, bias)
            top = jnp.max(s, axis=1, keepdims=True)
            if step == 0:
                top = jnp.broadcast_to(top, (ROWS, HD))
                acc[h] = product(numerators(s, top), lo, count)
            else:
                old = peak[h]
                top = jnp.maximum(old, top)
                fade = jnp.exp2((old - top) * LOG2)
                got = product(numerators(s, top), lo, count)
                acc[h, :, :HD] = acc[h, :, :HD] * fade + got[:, :HD]
                acc[h, :, HD:] = acc[h, :, HD:] * fade + got[:, HD:]
            peak[h] = top
            for item in RELAYS.get((step, h), ()):
                carry_on(item)

    def answer(n):
        a_half, h0, h1 = ANSWERS[n]
        who = (2 * x + yh, z * YS + 2 * c + a_half)
        here = jnp.logical_and(mine, yl == a_half)
        width = (h1 - h0) * HD
        cols = pl.ds(pl.multiple_of(yl * WIDE + h0 * HD, 128), width)
        src = obuf.at[a_half, :, pl.ds(h0 * HD, width)]
        return (src, out.at[0, :, cols], o_send.at[n], o_recv, who, here)

    take_window()
    from_sibling(7)
    pieces = [piece for half in (c, 1 - c) for piece in prompt_bias(7, half)]
    late = jnp.broadcast_to(jnp.concatenate(pieces, axis=1), (128, CHUNK))
    for a_half in range(2):
        rows = slice(a_half * 128, a_half * 128 + 128)
        if a_half == 0:
            lo = TAIL
            bias = jnp.concatenate([bias0[rows, 0:128], late, bias0[rows, 128:640]], axis=1)
        else:
            lo = TAIL + 128
            bias = jnp.concatenate([late, bias0[rows, 128:]], axis=1)
        count = CHUNK + 640
        for h in range(HG):
            s = weigh(lo, count, rows, h, bias)
            old = peak[h, rows, :]
            top = jnp.maximum(old, jnp.max(s, axis=1, keepdims=True))
            fade = jnp.exp2((old - top) * LOG2)
            got = product(numerators(s, top), lo, count)
            weighted = acc[h, rows, :HD] * fade + got[:, :HD]
            total = acc[h, rows, HD:] * fade + got[:, HD:]
            obuf[a_half, :, h * HD:(h + 1) * HD] = (weighted / total).astype(jnp.bfloat16)
            for n, (half, _, stop) in enumerate(ANSWERS):
                if (half, stop) == (a_half, h + 1):
                    put(*answer(n))

    for n in range(len(ANSWERS)):
        sent(*answer(n))
    for h in range(2):
        for item in staged(h):
            sent(*item)

    def settle(i, carry):
        for item in queried(i):
            sent(*item)
        return carry

    lax.fori_loop(0, 16, settle, 0)
    for r in range(ZS):
        for kind in range(2):
            for part in range(2):
                for copy in onward(kind, part, r):
                    copy.wait_send()
    for copy in forwards() + crossings():
        copy.wait_send()
    arrived(out, o_recv)


def body(
    prompt_keys, prompt_values, resp_queries, resp_keys, resp_values, segment_ids, prompt_lengths
):
    dma = pltpu.SemaphoreType.DMA
    held = pl.BlockSpec(memory_space=pl.ANY)
    return pl.pallas_call(
        kernel,
        out_shape=jax.ShapeDtypeStruct((1, 128, H * HD), jnp.bfloat16),
        in_specs=[held] * 5
        + [pl.BlockSpec(memory_space=pltpu.VMEM), pl.BlockSpec(memory_space=pltpu.SMEM)],
        out_specs=held,
        scratch_shapes=[
            pltpu.VMEM((ROWS, WIDE), jnp.bfloat16),
            pltpu.VMEM((KEYS, HD), jnp.bfloat16),
            pltpu.VMEM((KEYS, 2 * HD), jnp.bfloat16),
            pltpu.VMEM((8, 128), jnp.int32),
            pltpu.VMEM((3, 2, 8, 128), jnp.int32),
            pltpu.VMEM((HG, ROWS, 2 * HD), jnp.float32),
            pltpu.VMEM((HG, ROWS, HD), jnp.float32),
            pltpu.VMEM((2, 128, WIDE), jnp.bfloat16),
            pltpu.VMEM((ROWS, WIN), jnp.float32),
            dma((3, 16)),
            dma,
            dma((2,)),
            dma((3, 2)),
            dma((3, 2)),
            dma((2, 2, ZS)),
            dma((2, 2, ZS)),
            dma((2, 2, ZS)),
            dma((2, 2, ZS)),
            dma((3, 4)),
            dma((3, 4)),
            dma((len(ANSWERS),)),
            dma,
        ],
        compiler_params=pltpu.CompilerParams(
            collective_id=0, has_side_effects=True, vmem_limit_bytes=60 << 20
        ),
        name="shared_prompt_attention",
    )(prompt_keys, prompt_values, resp_queries, resp_keys, resp_values, segment_ids, prompt_lengths)


def solution(mesh):
    in_specs = (
        P("grp", "seq", None),
        P("grp", "seq", None),
        P(None, ("seq", "grp"), None),
        P(None, ("seq", "grp"), None),
        P(None, ("seq", "grp"), None),
        P("grp", "seq"),
        P("grp"),
    )
    out_specs = P("grp", "seq", None)
    return jax.shard_map(body, mesh=mesh, in_specs=in_specs, out_specs=out_specs, check_vma=False)
```

time: 80.7 us -> 64.7 us (0.80)
  Pallas kernels: 74.5 us -> 62.1 us
  local copies, waits for them, and re-layouts: 5.27 us -> 1.82 us
    pallas_call x1, Pallas kernels: 74.5 us -> 62.1 us  [body(): pl.pallas_call(kernel, out_shape=jax.ShapeDtypeStruct((1, 128, H * HD), j...]
    unnamed x13 -> x1, local copies, waits for them, and re-layouts: 5.27 us -> 1.82 us
where the time goes in v2:
time: 64.7 us; the launch traced here: 64.6 us
  Pallas kernels  62.1 us (96%)
  local copies, waits for them, and re-layouts  1.82 us (3%)
  between operations  0.66 us (1%)
    pallas_call x1, Pallas kernels, body(): pl.pallas_call(kernel, out_shape=jax.ShapeDtypeStruct((1, 128, H * HD), j...  62.1 us
    unnamed x1, local copies, waits for them, and re-layouts  1.82 us

profile of v2, /device:TPU:24, one launch (start us, length us, event | category | flops | bytes accessed | tf_op | source)
XLA Modules:
  0.0 64.6 jit_solution(5780589191387230352)
XLA Ops:
  0.7 62.1 %shared_prompt_attention.1 = bf16[1,128,1792]{2,1,0:T(8,128)(2,1)} custom-call(bf16[1,256,256]{2,1,0:T(8,128)(2,1)} %pk.1, bf16[1,256,256]{2,1,0:T(8,128)(2,1)} %pv.1, bf16[8,16,1792]{2,1,0:T(8,128)(2,1)} %rq.1, bf16[8,16,256]{2,1,0:T(8,128)(2,1)} %rk.1, bf16[8,16,256]{2,1,0:T(8,128)(2,1)} %rv.1, s32[1,128]{1,0:T(1,128)} %seg.1, s32[1]{0:T(128)S(6)} %copy.9.plen), custom_call_target="tpu_custom_call" | custom-call | tf_op jit(solution)/shard_map/shared_prompt_attention/pallas_call | solution.py:393
  62.8 1.8 %copy.10 = bf16[1,128,1792]{2,1,0:T(8,128)(2,1)} copy(bf16[1,128,1792]{2,1,0:T(8,128)(2,1)} %shared_prompt_attention.1) | data formatting | bytes 917504

commit v3 on v2

--- a/solution.py
+++ b/solution.py
@@ -41,8 +41,8 @@
 RELAYS = {
     (0, 3): moves_of(VALUE_PARTS, 1, 2),
     (1, 5): moves_of(PARTS, 3, 4) + ("send",),
-    (2, 5): moves_of(PARTS, 5, 6),
-    (3, 4): ("cross",) + moves_of(PARTS, 7),
+    (2, 5): moves_of(PARTS, 5, 6) + ("cross",),
+    (3, 4): moves_of(PARTS, 7) + ("take",),
 }
 ANSWERS = ((0, 0, 7), (1, 0, 4), (1, 4, 7))
 MESH = pl.DeviceIdType.MESH
@@ -292,6 +292,8 @@
             send_window()
         elif item == "cross":
             cross_window()
+        elif item == "take":
+            take_window()
         else:
             relay(*item)
 
@@ -337,7 +339,6 @@
         src = obuf.at[a_half, :, pl.ds(h0 * HD, width)]
         return (src, out.at[0, :, cols], o_send.at[n], o_recv, who, here)
 
-    take_window()
     from_sibling(7)
     pieces = [piece for half in (c, 1 - c) for piece in prompt_bias(7, half)]
     late = jnp.broadcast_to(jnp.concatenate(pieces, axis=1), (128, CHUNK))

time: 64.7 us -> 67.5 us (1.043)
  Pallas kernels: 62.1 us -> 64.9 us
    pallas_call x1, Pallas kernels: 62.1 us -> 64.9 us  [body(): pl.pallas_call(kernel, out_shape=jax.ShapeDtypeStruct((1, 128, H * HD), j...]
where the time goes in v3:
time: 67.5 us; the launch traced here: 67.4 us
  Pallas kernels  64.9 us (96%)
  local copies, waits for them, and re-layouts  1.82 us (3%)
    pallas_call x1, Pallas kernels, body(): pl.pallas_call(kernel, out_shape=jax.ShapeDtypeStruct((1, 128, H * HD), j...  64.9 us
    unnamed x1, local copies, waits for them, and re-layouts  1.82 us

profile of v3, /device:TPU:24, one launch (start us, length us, event | category | flops | bytes accessed | tf_op | source)
XLA Modules:
  0.0 67.4 jit_solution(1070383340487697527)
XLA Ops:
  0.7 64.9 %shared_prompt_attention.1 = bf16[1,128,1792]{2,1,0:T(8,128)(2,1)} custom-call(bf16[1,256,256]{2,1,0:T(8,128)(2,1)} %pk.1, bf16[1,256,256]{2,1,0:T(8,128)(2,1)} %pv.1, bf16[8,16,1792]{2,1,0:T(8,128)(2,1)} %rq.1, bf16[8,16,256]{2,1,0:T(8,128)(2,1)} %rk.1, bf16[8,16,256]{2,1,0:T(8,128)(2,1)} %rv.1, s32[1,128]{1,0:T(1,128)} %seg.1, s32[1]{0:T(128)S(6)} %copy.9.plen), custom_call_target="tpu_custom_call" | custom-call | tf_op jit(solution)/shard_map/shared_prompt_attention/pallas_call | solution.py:394
  65.5 1.8 %copy.10 = bf16[1,128,1792]{2,1,0:T(8,128)(2,1)} copy(bf16[1,128,1792]{2,1,0:T(8,128)(2,1)} %shared_prompt_attention.1) | data formatting | bytes 917504
